TPU v7x, 512 devices: a whole 4x8x8 slice. The times are simulated.
512 devices in a mesh: seq: 64 (over y, x, core), tp: 8 (over z).
Axes of the slice: x: 4, y: 8, z: 8, core: 2. Of those that a mesh axis runs over, the one named last changes fastest.
Arguments:
- queries: bfloat16 [32768, 4096], P('seq', 'tp'), may hold values from -9 to 9
- keys: bfloat16 [32768, 4096], P('seq', 'tp'), may hold values from -9 to 9
- values: bfloat16 [32768, 4096], P('seq', 'tp'), may hold values from -6 to 6
- route: int32 [32, 32768], P('tp', 'seq'), may hold values from 0 to 32767, as said below
- members: int32 [32, 32768], P('tp', 'seq'), may hold values from 0 to 32767, as said below
- pattern: int32 [32, 128, 10], P('tp', 'seq'), may hold values from 0 to 1, as said below
- w_out: bfloat16 [4096, 4096], P('tp', 'seq'), may hold values from -0.25 to 0.25
Outputs:
- mixed: bfloat16 [32768, 4096], P('seq', 'tp')
Inputs may be any that keep to these rules, and one draw needn't show every extreme that they name: `route`: each row is a permutation of the positions; for every aligned block of 512 positions and every aligned block of 512 slots, exactly 8 of the block's positions have their slot in that slot block. members[h] is the inverse permutation of route[h]: members[h, route[h, p]] = p. `pattern`: entries 2 * 2 and 2 * 2 + 1 (the cluster's own blocks) are always 1; entries whose cluster lies outside 0 to 127 are always 0.
All inputs are finite; a program needn't handle non-finite values.
Results may differ from a plain program's by a relative error of at most 0.017.
Values may be sent and summed in bfloat16 or wider, within the bound.
A program may use at most 64 MiB of HBM per device.

v0:
```python
import jax
import jax.numpy as jnp
from jax import lax
from jax.sharding import PartitionSpec as P

CLUSTER = 256
REACH = 2


def extended_2(cells, sides, width):
    for axis, dim in sides:
        count = lax.axis_size(axis)
        ends = count - 1
        head = lax.slice_in_dim(cells, 0, width, axis=dim)
        tail = lax.slice_in_dim(cells, cells.shape[dim] - width, cells.shape[dim], axis=dim)
        cells = jnp.concatenate(
            [
                lax.ppermute(tail, axis, [(i, (i + 1) % count) for i in range(ends)]),
                cells,
                lax.ppermute(head, axis, [((i + 1) % count, i) for i in range(ends)]),
            ],
            axis=dim,
        )
    return cells


def attend_head(pieces):
    query_rows, key_rows, value_rows, pattern_rows = pieces
    head_width = query_rows.shape[1]
    cluster_count = query_rows.shape[0] // CLUSTER
    window_rows = (2 * REACH + 1) * CLUSTER
    starts = jnp.arange(cluster_count) * CLUSTER
    key_window = jax.vmap(
        lambda slot_start: lax.dynamic_slice_in_dim(key_rows, slot_start, window_rows, 0)
    )(starts)
    value_window = jax.vmap(
        lambda slot_start: lax.dynamic_slice_in_dim(value_rows, slot_start, window_rows, 0)
    )(starts)
    query_blocks = query_rows.reshape(cluster_count, CLUSTER, head_width)
    scores = jnp.einsum(
        "cqd,ckd->cqk", query_blocks, key_window, preferred_element_type=jnp.float32
    ) * head_width ** (-0.5)
    allowed = jnp.repeat(pattern_rows, CLUSTER // 2, axis=1) > 0
    scores = jnp.where(allowed[:, None, :], scores, -jnp.inf)
    row_max = jnp.max(scores, axis=-1, keepdims=True)
    exponent = jnp.exp(scores - row_max)
    weights = (exponent / jnp.sum(exponent, axis=-1, keepdims=True)).astype(jnp.bfloat16)
    context = jnp.einsum(
        "cqk,ckd->cqd", weights, value_window, preferred_element_type=jnp.float32
    ).astype(jnp.bfloat16)
    return context.reshape(query_rows.shape[0], head_width)


def buffer_index(group_of, order_key, per_peer):
    same_group = group_of[:, :, None] == group_of[:, None, :]
    earlier = order_key[:, None, :] < order_key[:, :, None]
    rank = jnp.sum((same_group & earlier).astype(jnp.int32), axis=2)
    return group_of * per_peer + rank


def shards(queries, keys, values, route, members, pattern, w_out):
    rows_here = queries.shape[0]
    head_count = route.shape[0]
    head_width = queries.shape[1] // head_count
    peer_count = lax.axis_size("seq")
    per_peer = rows_here // peer_count
    local_iota = jnp.arange(rows_here, dtype=jnp.int32)
    send_index = buffer_index(route // rows_here, route, per_peer)
    local_slots = jnp.broadcast_to(local_iota[None, :], members.shape)
    arrival_index = buffer_index(members // rows_here, local_slots, per_peer)
    send_table = (send_index[:, None, :] == local_iota[None, :, None]).astype(jnp.bfloat16)
    land_table = (arrival_index[:, :, None] == local_iota[None, None, :]).astype(jnp.bfloat16)
    stacked = jnp.concatenate(
        [
            queries.reshape(rows_here, head_count, head_width),
            keys.reshape(rows_here, head_count, head_width),
            values.reshape(rows_here, head_count, head_width),
        ],
        axis=2,
    )
    packed = jnp.einsum(
        "hap,phd->had", send_table, stacked, preferred_element_type=jnp.float32
    ).astype(jnp.bfloat16)

    def outgoing(column_index):
        part_rows = packed[:, :, column_index * head_width : (column_index + 1) * head_width]
        return part_rows.reshape(head_count, peer_count, per_peer, head_width)

    sent_query, sent_key, sent_value = (
        lax.all_to_all(outgoing(0), "seq", split_axis=1, concat_axis=1, tiled=True),
        lax.all_to_all(outgoing(1), "seq", split_axis=1, concat_axis=1, tiled=True),
        lax.all_to_all(outgoing(2), "seq", split_axis=1, concat_axis=1, tiled=True),
    )
    arrived = jnp.concatenate(
        [
            sent_query.reshape(head_count, rows_here, head_width),
            sent_key.reshape(head_count, rows_here, head_width),
            sent_value.reshape(head_count, rows_here, head_width),
        ],
        axis=2,
    )
    placed = jnp.einsum(
        "hsa,had->hsd", land_table, arrived, preferred_element_type=jnp.float32
    ).astype(jnp.bfloat16)
    ordered_query = placed[:, :, :head_width]
    keys_values = jnp.stack(
        [placed[:, :, head_width : 2 * head_width], placed[:, :, 2 * head_width :]]
    )
    extended = extended_2(keys_values, (("seq", 2),), REACH * CLUSTER)
    context = lax.map(attend_head, (ordered_query, extended[0], extended[1], pattern))
    returning = jnp.einsum(
        "hsa,hsd->had", land_table, context, preferred_element_type=jnp.float32
    ).astype(jnp.bfloat16)
    returning = returning.reshape(head_count, peer_count, per_peer, head_width)
    returned = lax.all_to_all(returning, "seq", split_axis=1, concat_axis=1, tiled=True).reshape(
        head_count, rows_here, head_width
    )
    attended = jnp.einsum(
        "hap,had->phd", send_table, returned, preferred_element_type=jnp.float32
    ).astype(jnp.bfloat16)
    attended = attended.reshape(rows_here, head_count * head_width)
    partial_value = jnp.dot(
        attended,
        lax.all_gather(w_out, "seq", axis=1, tiled=True),
        preferred_element_type=jnp.float32,
    )
    column_count = partial_value.shape[1] // lax.axis_size("tp")
    summed = lax.psum(partial_value.astype(jnp.bfloat16), "tp").astype(jnp.float32)
    mixed_out = lax.dynamic_slice_in_dim(
        summed, lax.axis_index("tp") * column_count, column_count, 1
    )
    return mixed_out.astype(jnp.bfloat16)


def solution(mesh):
    placed = (
        P("seq", "tp"),
        P("seq", "tp"),
        P("seq", "tp"),
        P("tp", "seq"),
        P("tp", "seq"),
        P("tp", "seq", None),
        P("tp", "seq"),
    )
    return jax.shard_map(
        shards, mesh=mesh, in_specs=placed, out_specs=P("seq", "tp"), check_vma=False
    )
```

profile of v0, /device:TPU:1, one launch (start us, length us, event | category | flops | bytes accessed | tf_op | source)
XLA Modules:
  0.0 320.6 jit_solution(11738363935786757012)
XLA Ops:
  7.3 1.8 convert_reduce_fusion
  16.0 11.6 %all-to-all-start.2 = ((bf16[4,64,8,128]{3,2,0,1:T(8,128)(2,1)}), bf16[4,64,8,128]{3,2,0,1:T(8,128)(2,1)S(1)}, u32[]{:S(2)}, u32[]{:S(2)}) async-start(bf16[4,64,8,128]{3,2,0,1:T(8,128)(2,1)} %copy.44), calls=%async_computation.2 | async-start | bytes 1048576 | tf_op jit(solution)/shard_map/all_to_all | solution.py:92
  28.5 16.8 %all-to-all-done.2 = bf16[4,64,8,128]{3,2,0,1:T(8,128)(2,1)S(1)} async-done(((bf16[4,64,8,128]{3,2,0,1:T(8,128)(2,1)}), bf16[4,64,8,128]{3,2,0,1:T(8,128)(2,1)S(1)}, u32[]{:S(2)}, u32[]{:S(2)}) %all-to-all-start.2) | async-done | bytes 524320 | tf_op jit(solution)/shard_map/all_to_all | solution.py:92
  45.3 5.7 %all-to-all-start.1 = ((bf16[4,64,8,128]{3,2,0,1:T(8,128)(2,1)}), bf16[4,64,8,128]{3,2,0,1:T(8,128)(2,1)S(1)}, u32[]{:S(2)}, u32[]{:S(2)}) async-start(bf16[4,64,8,128]{3,2,0,1:T(8,128)(2,1)} %copy.42), calls=%async_computation.1 | async-start | bytes 1048576 | tf_op jit(solution)/shard_map/all_to_all | solution.py:91
  51.9 16.8 %all-to-all-done.1 = bf16[4,64,8,128]{3,2,0,1:T(8,128)(2,1)S(1)} async-done(((bf16[4,64,8,128]{3,2,0,1:T(8,128)(2,1)}), bf16[4,64,8,128]{3,2,0,1:T(8,128)(2,1)S(1)}, u32[]{:S(2)}, u32[]{:S(2)}) %all-to-all-start.1) | async-done | bytes 524320 | tf_op jit(solution)/shard_map/all_to_all | solution.py:91
  68.8 5.7 %all-to-all-start = ((bf16[4,64,8,128]{3,2,0,1:T(8,128)(2,1)}), bf16[4,64,8,128]{3,2,0,1:T(8,128)(2,1)S(1)}, u32[]{:S(2)}, u32[]{:S(2)}) async-start(bf16[4,64,8,128]{3,2,0,1:T(8,128)(2,1)} %copy.40), calls=%async_computation | async-start | bytes 1048576 | tf_op jit(solution)/shard_map/all_to_all | solution.py:90
  76.1 16.1 %all-to-all-done = bf16[4,64,8,128]{3,2,0,1:T(8,128)(2,1)S(1)} async-done(((bf16[4,64,8,128]{3,2,0,1:T(8,128)(2,1)}), bf16[4,64,8,128]{3,2,0,1:T(8,128)(2,1)S(1)}, u32[]{:S(2)}, u32[]{:S(2)}) %all-to-all-start) | async-done | bytes 524320 | tf_op jit(solution)/shard_map/all_to_all | solution.py:90
  94.9 3.4 %collective-permute-start = (bf16[2,4,512,128]{3,2,1,0:T(8,128)(2,1)S(1)}, bf16[2,4,512,128]{3,2,1,0:T(8,128)(2,1)S(1)}, u32[]{:S(2)}, u32[]{:S(2)}) collective-permute-start(bf16[2,4,512,128]{3,2,1,0:T(8,128)(2,1)S(1)} %pad_maximum_fusion.1), channel_id=1, source_target_pairs={{0,8},{8,16},{16,24},{24,32},{32,40},{40,48},{48,56},{56,64},{64,7... | collective-permute-start | bytes 3145736 | tf_op jit(solution)/shard_map/ppermute | solution.py:18
  98.3 1.9 collective-permute-start.1
  100.5 9.5 %collective-permute-done = bf16[2,4,512,128]{3,2,1,0:T(8,128)(2,1)S(1)} collective-permute-done((bf16[2,4,512,128]{3,2,1,0:T(8,128)(2,1)S(1)}, bf16[2,4,512,128]{3,2,1,0:T(8,128)(2,1)S(1)}, u32[]{:S(2)}, u32[]{:S(2)}) %collective-permute-start) | collective-permute-done | bytes 1048608 | tf_op jit(solution)/shard_map/ppermute | solution.py:18
  110.0 4.5 %collective-permute-done.1 = bf16[2,4,512,128]{3,2,1,0:T(8,128)(2,1)} collective-permute-done((bf16[2,4,512,128]{3,2,1,0:T(8,128)(2,1)S(1)}, bf16[2,4,512,128]{3,2,1,0:T(8,128)(2,1)}, u32[]{:S(2)}, u32[]{:S(2)}) %collective-permute-start.1) | collective-permute-done | bytes 1048608 | tf_op jit(solution)/shard_map/ppermute | solution.py:20
  114.5 1.3 pad_maximum_fusion
  115.8 1.4 slice_bitcast_fusion
  117.2 27.3 %while.16 = (s32[]{:T(128)}, bf16[4,512,128]{2,1,0:T(8,128)(2,1)}, s32[4,2,10]{2,1,0:T(2,128)}, bf16[4,512,128]{2,1,0:T(8,128)(2,1)}, bf16[4,1536,128]{2,1,0:T(8...) while((s32[]{:T(128)}, bf16[4,512,128]{2,1,0:T(8,128)(2,1)}, ...), condition=%wide.region_5.6_spmd, body=%wide.region_2.5_spmd.sunk | while | flops 509283360 | bytes 7096867 | solution.py:110
  122.0 1.4 fusion.66
  128.8 1.4 fusion.66
  135.6 1.4 fusion.66
  142.4 1.4 fusion.66
  144.5 1.8 fusion.35
  146.5 31.2 %all_to_all.20 = bf16[4,64,8,128]{3,2,0,1:T(8,128)(2,1)S(1)} all-to-all(bf16[4,64,8,128]{3,2,0,1:T(8,128)(2,1)S(1)} %copy.47), channel_id=1, replica_groups=mesh['seq'=64,'tp'=8] {'seq'}, dimensions={1} | all-to-all | bytes 1048576 | tf_op jit(solution)/shard_map/all_to_all | solution.py:115
  178.6 11.8 %all-gather.2.cloned.1.call-done = bf16[512,4096]{0,1:T(8,128)(2,1)} async-done(((bf16[512,64]{0,1:T(8,128)(2,1)}), bf16[512,4096]{0,1:T(8,128)(2,1)}) %all-gather.2.cloned.1.call-update) | async-done | bytes 4194320 | tf_op jit(solution)/shard_map/all_gather | solution.py:124
  190.3 6.6 %convolution_convert_fusion = bf16[512,4096]{1,0:T(8,128)(2,1)} fusion(bf16[512,512]{0,1:T(8,128)(2,1)S(1)} %bitcast.112, bf16[512,4096]{0,1:T(8,128)(2,1)} %all-gather.2.cloned.1.call-done), kind=kOutput, calls=%fused_computation.26 | convolution fusion | flops 2149580800 | bytes 8912896 | tf_op jit(solution)/shard_map/dot_general | solution.py:122
  196.9 115.0 %all-reduce.3.cloned.1.call-done = bf16[512,4096]{1,0:T(8,128)(2,1)} async-done(((bf16[512,4096]{1,0:T(8,128)(2,1)}), bf16[512,4096]{1,0:T(8,128)(2,1)}) %all-reduce.3.cloned.1.call-update) | async-done | bytes 4194320 | tf_op jit(solution)/shard_map/psum | solution.py:128
  311.9 1.9 convert_convert_fusion
  (118 shorter events, 39.0 us)
Async XLA Ops:
  6.5 6.4 %copy-start = (bf16[512,512]{1,0:T(8,128)(2,1)S(1)}, bf16[512,512]{1,0:T(8,128)(2,1)}, u32[]{:S(2)}) copy-start(bf16[512,512]{1,0:T(8,128)(2,1)} %param.11) | copy-start | bytes 1572868
  15.1 59.6 %copy-start.1 = (s32[4,512]{1,0:T(4,128)S(1)}, s32[4,512]{1,0:T(4,128)}, u32[]{:S(2)}) copy-start(s32[4,512]{1,0:T(4,128)} %param.13) | copy-start | bytes 24580
  16.0 29.3 %all-to-all-start.2 = ((bf16[4,64,8,128]{3,2,0,1:T(8,128)(2,1)}), bf16[4,64,8,128]{3,2,0,1:T(8,128)(2,1)S(1)}, u32[]{:S(2)}, u32[]{:S(2)}) async-start(bf16[4,64,8,128]{3,2,0,1:T(8,128)(2,1)} %copy.44), calls=%async_computation.2 | async-start | bytes 1048576 | tf_op jit(solution)/shard_map/all_to_all | solution.py:92
  45.3 23.4 %all-to-all-start.1 = ((bf16[4,64,8,128]{3,2,0,1:T(8,128)(2,1)}), bf16[4,64,8,128]{3,2,0,1:T(8,128)(2,1)S(1)}, u32[]{:S(2)}, u32[]{:S(2)}) async-start(bf16[4,64,8,128]{3,2,0,1:T(8,128)(2,1)} %copy.42), calls=%async_computation.1 | async-start | bytes 1048576 | tf_op jit(solution)/shard_map/all_to_all | solution.py:91
  68.8 23.4 %all-to-all-start = ((bf16[4,64,8,128]{3,2,0,1:T(8,128)(2,1)}), bf16[4,64,8,128]{3,2,0,1:T(8,128)(2,1)S(1)}, u32[]{:S(2)}, u32[]{:S(2)}) async-start(bf16[4,64,8,128]{3,2,0,1:T(8,128)(2,1)} %copy.40), calls=%async_computation | async-start | bytes 1048576 | tf_op jit(solution)/shard_map/all_to_all | solution.py:90
  74.5 115.8 %all-gather.2.cloned.1.call-start = ((), (), s32[]{:S(2)}) async-start(), calls=%async_computation.4 | async-start | bytes 4259840 | tf_op jit(solution)/shard_map/all_gather | solution.py:124
  94.9 15.1 %collective-permute-start = (bf16[2,4,512,128]{3,2,1,0:T(8,128)(2,1)S(1)}, bf16[2,4,512,128]{3,2,1,0:T(8,128)(2,1)S(1)}, u32[]{:S(2)}, u32[]{:S(2)}) collective-permute-start(bf16[2,4,512,128]{3,2,1,0:T(8,128)(2,1)S(1)} %pad_maximum_fusion.1), channel_id=1, source_target_pairs={{0,8},{8,16},{16,24},{24,32},{32,40},{40,48},{48,56},{56,64},{64,7... | collective-permute-start | bytes 3145736 | tf_op jit(solution)/shard_map/ppermute | solution.py:18
  98.3 16.2 %collective-permute-start.1 = (bf16[2,4,512,128]{3,2,1,0:T(8,128)(2,1)S(1)}, bf16[2,4,512,128]{3,2,1,0:T(8,128)(2,1)}, u32[]{:S(2)}, u32[]{:S(2)}) collective-permute-start(bf16[2,4,512,128]{3,2,1,0:T(8,128)(2,1)S(1)} %pad_maximum_fusion.1), channel_id=1, source_target_pairs={{8,0},{16,8},{24,16},{32,24},{40,32},{48,40},{56,48},{64,56},{72,6... | collective-permute-start | bytes 3145736 | tf_op jit(solution)/shard_map/ppermute | solution.py:20
  100.2 211.7 %all-reduce.3.cloned.1.call-start = ((), (), s32[]{:S(2)}) async-start(), calls=%async_computation.5 | async-start | bytes 8388608 | tf_op jit(solution)/shard_map/psum | solution.py:128
Sparse Core Ops, SparseCore 0:
  100.3 89.9 all-gather.1
  197.0 114.7 all-reduce.2
where the time goes:
time: 322 us; the launch traced here: 321 us
  waiting for transfers between devices  191 us (59%)
  blocking collectives  31.2 us (10%)
  starting transfers between devices  28.6 us (9%)
  local copies, waits for them, and re-layouts  23.8 us (7%)
  matrix products  21.4 us (7%)
  between operations  13.6 us (4%)
  other arithmetic  10.7 us (3%)
    psum x1, waiting for transfers between devices, shards(): lax.psum(partial_value.astype(jnp.bfloat16), 'tp').astype(jnp.float32)  115 us
    all_to_all x1, blocking collectives, shards(): lax.all_to_all(returning, 'seq', split_axis=1, concat_axis=1, tiled=True)  31.2 us
    all_to_all x1, waiting for transfers between devices, shards(): lax.all_to_all(outgoing(2), 'seq', split_axis=1, concat_axis=1, tiled=True)  16.8 us
    all_to_all x1, waiting for transfers between devices, shards(): lax.all_to_all(outgoing(1), 'seq', split_axis=1, concat_axis=1, tiled=True)  16.8 us
    all_to_all x1, waiting for transfers between devices, shards(): lax.all_to_all(outgoing(0), 'seq', split_axis=1, concat_axis=1, tiled=True)  16.1 us
    all_gather x1, waiting for transfers between devices, shards(): lax.all_gather(w_out, 'seq', axis=1, tiled=True)  11.8 us
    all_to_all x1, starting transfers between devices, shards(): lax.all_to_all(outgoing(2), 'seq', split_axis=1, concat_axis=1, tiled=True)  11.6 us
    ppermute x1, waiting for transfers between devices, extended_2(): lax.ppermute(tail, axis, [(i, (i + 1) % count) for i in range(ends)])  9.53 us
  transfers between devices with their start and end apart: 7, of which 7 were waited for; matrix products, arithmetic and copies ran while one was open for 11% of the time, Pallas kernels for 0%

commit v1 on v0

--- a/solution.py
+++ b/solution.py
@@ -125,7 +125,9 @@
         preferred_element_type=jnp.float32,
     )
     column_count = partial_value.shape[1] // lax.axis_size("tp")
-    summed = lax.psum(partial_value.astype(jnp.bfloat16), "tp").astype(jnp.float32)
+    summed = jnp.sum(lax.all_gather(partial_value.astype(jnp.bfloat16), "tp"), axis=0).astype(
+        jnp.float32
+    )
     mixed_out = lax.dynamic_slice_in_dim(
         summed, lax.axis_index("tp") * column_count, column_count, 1
     )

time: 322 us -> 554 us (1.72)
  waiting for transfers between devices: 191 us -> 409 us
  other arithmetic: 10.7 us -> 24.9 us
    all_gather x0 -> x1, waiting for transfers between devices: none -> 333 us  [shards(): lax.all_gather(partial_value.astype(jnp.bfloat16), 'tp')]
    psum x1 -> x0, waiting for transfers between devices: 115 us -> none  [shards(): lax.psum(partial_value.astype(jnp.bfloat16), 'tp').astype(jnp.float32)]
    reduce_sum x0 -> x1, other arithmetic: none -> 14.2 us  [shards(): jnp.sum(lax.all_gather(partial_value.astype(jnp.bfloat16), 'tp'), axis=0)]
  transfers between devices with their start and end apart: 7 -> 7, of which waited for: 7 -> 7; matrix products, arithmetic and copies ran while one was open for 11% -> 6% of each run, Pallas kernels for 0% -> 0%
where the time goes in v1:
time: 554 us; the launch traced here: 553 us
  waiting for transfers between devices  409 us (74%)
  blocking collectives  31.3 us (6%)
  starting transfers between devices  28.6 us (5%)
  other arithmetic  24.9 us (4%)
  local copies, waits for them, and re-layouts  23.7 us (4%)
  matrix products  21.4 us (4%)
  between operations  13.6 us (2%)
    all_gather x1, waiting for transfers between devices, shards(): lax.all_gather(partial_value.astype(jnp.bfloat16), 'tp')  333 us
    all_to_all x1, blocking collectives, shards(): lax.all_to_all(returning, 'seq', split_axis=1, concat_axis=1, tiled=True)  31.3 us
    all_to_all x1, waiting for transfers between devices, shards(): lax.all_to_all(outgoing(2), 'seq', split_axis=1, concat_axis=1, tiled=True)  16.8 us
    all_to_all x1, waiting for transfers between devices, shards(): lax.all_to_all(outgoing(1), 'seq', split_axis=1, concat_axis=1, tiled=True)  16.8 us
    all_to_all x1, waiting for transfers between devices, shards(): lax.all_to_all(outgoing(0), 'seq', split_axis=1, concat_axis=1, tiled=True)  16.1 us
    reduce_sum x1, other arithmetic, shards(): jnp.sum(lax.all_gather(partial_value.astype(jnp.bfloat16), 'tp'), axis=0)  14.2 us
    all_gather x1, waiting for transfers between devices, shards(): lax.all_gather(w_out, 'seq', axis=1, tiled=True)  11.7 us
    all_to_all x1, starting transfers between devices, shards(): lax.all_to_all(outgoing(2), 'seq', split_axis=1, concat_axis=1, tiled=True)  11.6 us
  transfers between devices with their start and end apart: 7, of which 7 were waited for; matrix products, arithmetic and copies ran while one was open for 6% of the time, Pallas kernels for 0%

profile of v1, /device:TPU:1, one launch (start us, length us, event | category | flops | bytes accessed | tf_op | source)
XLA Modules:
  0.0 552.9 jit_solution(14440029219832825550)
XLA Ops:
  7.3 1.8 convert_reduce_fusion
  15.9 11.6 %all-to-all-start.2 = ((bf16[4,64,8,128]{3,2,0,1:T(8,128)(2,1)}), bf16[4,64,8,128]{3,2,0,1:T(8,128)(2,1)S(1)}, u32[]{:S(2)}, u32[]{:S(2)}) async-start(bf16[4,64,8,128]{3,2,0,1:T(8,128)(2,1)} %copy.44), calls=%async_computation.2 | async-start | bytes 1048576 | tf_op jit(solution)/shard_map/all_to_all | solution.py:92
  28.4 16.8 %all-to-all-done.2 = bf16[4,64,8,128]{3,2,0,1:T(8,128)(2,1)S(1)} async-done(((bf16[4,64,8,128]{3,2,0,1:T(8,128)(2,1)}), bf16[4,64,8,128]{3,2,0,1:T(8,128)(2,1)S(1)}, u32[]{:S(2)}, u32[]{:S(2)}) %all-to-all-start.2) | async-done | bytes 524320 | tf_op jit(solution)/shard_map/all_to_all | solution.py:92
  45.2 5.7 %all-to-all-start.1 = ((bf16[4,64,8,128]{3,2,0,1:T(8,128)(2,1)}), bf16[4,64,8,128]{3,2,0,1:T(8,128)(2,1)S(1)}, u32[]{:S(2)}, u32[]{:S(2)}) async-start(bf16[4,64,8,128]{3,2,0,1:T(8,128)(2,1)} %copy.42), calls=%async_computation.1 | async-start | bytes 1048576 | tf_op jit(solution)/shard_map/all_to_all | solution.py:91
  51.8 16.8 %all-to-all-done.1 = bf16[4,64,8,128]{3,2,0,1:T(8,128)(2,1)S(1)} async-done(((bf16[4,64,8,128]{3,2,0,1:T(8,128)(2,1)}), bf16[4,64,8,128]{3,2,0,1:T(8,128)(2,1)S(1)}, u32[]{:S(2)}, u32[]{:S(2)}) %all-to-all-start.1) | async-done | bytes 524320 | tf_op jit(solution)/shard_map/all_to_all | solution.py:91
  68.7 5.7 %all-to-all-start = ((bf16[4,64,8,128]{3,2,0,1:T(8,128)(2,1)}), bf16[4,64,8,128]{3,2,0,1:T(8,128)(2,1)S(1)}, u32[]{:S(2)}, u32[]{:S(2)}) async-start(bf16[4,64,8,128]{3,2,0,1:T(8,128)(2,1)} %copy.40), calls=%async_computation | async-start | bytes 1048576 | tf_op jit(solution)/shard_map/all_to_all | solution.py:90
  76.0 16.1 %all-to-all-done = bf16[4,64,8,128]{3,2,0,1:T(8,128)(2,1)S(1)} async-done(((bf16[4,64,8,128]{3,2,0,1:T(8,128)(2,1)}), bf16[4,64,8,128]{3,2,0,1:T(8,128)(2,1)S(1)}, u32[]{:S(2)}, u32[]{:S(2)}) %all-to-all-start) | async-done | bytes 524320 | tf_op jit(solution)/shard_map/all_to_all | solution.py:90
  94.8 3.4 collective-permute-start
  98.2 1.9 collective-permute-start.1
  100.4 9.5 %collective-permute-done = bf16[2,4,512,128]{3,2,1,0:T(8,128)(2,1)S(1)} collective-permute-done((bf16[2,4,512,128]{3,2,1,0:T(8,128)(2,1)S(1)}, bf16[2,4,512,128]{3,2,1,0:T(8,128)(2,1)S(1)}, u32[]{:S(2)}, u32[]{:S(2)}) %collective-permute-start) | collective-permute-done | bytes 1048608 | tf_op jit(solution)/shard_map/ppermute | solution.py:18
  109.9 4.5 collective-permute-done.1
  115.7 1.4 slice_bitcast_fusion
  117.1 27.3 %while.16 = (s32[]{:T(128)}, bf16[4,512,128]{2,1,0:T(8,128)(2,1)}, s32[4,2,10]{2,1,0:T(2,128)}, bf16[4,512,128]{2,1,0:T(8,128)(2,1)}, bf16[4,1536,128]{2,1,0:T(8...) while((s32[]{:T(128)}, bf16[4,512,128]{2,1,0:T(8,128)(2,1)}, ...), condition=%wide.region_5.6_spmd, body=%wide.region_2.5_spmd.sunk | while | flops 509283360 | bytes 7096867 | solution.py:110
  121.9 1.4 fusion.66
  128.7 1.4 fusion.66
  135.5 1.4 fusion.66
  142.3 1.4 fusion.66
  144.4 1.8 fusion.35
  146.3 31.3 %all_to_all.20 = bf16[4,64,8,128]{3,2,0,1:T(8,128)(2,1)S(1)} all-to-all(bf16[4,64,8,128]{3,2,0,1:T(8,128)(2,1)S(1)} %copy.47), channel_id=1, replica_groups=mesh['seq'=64,'tp'=8] {'seq'}, dimensions={1} | all-to-all | bytes 1048576 | tf_op jit(solution)/shard_map/all_to_all | solution.py:115
  178.5 11.7 %all-gather.4.cloned.1.call-done = bf16[512,4096]{0,1:T(8,128)(2,1)} async-done(((bf16[512,64]{0,1:T(8,128)(2,1)}), bf16[512,4096]{0,1:T(8,128)(2,1)}) %all-gather.4.cloned.1.call-update) | async-done | bytes 4194320 | tf_op jit(solution)/shard_map/all_gather | solution.py:124
  190.2 6.6 %convolution_convert_fusion = bf16[512,4096]{1,0:T(8,128)(2,1)} fusion(bf16[512,512]{0,1:T(8,128)(2,1)S(1)} %bitcast.114, bf16[512,4096]{0,1:T(8,128)(2,1)} %all-gather.4.cloned.1.call-done), kind=kOutput, calls=%fused_computation.26 | convolution fusion | flops 2149580800 | bytes 8912896 | tf_op jit(solution)/shard_map/dot_general | solution.py:122
  196.9 333.1 %all-gather.6.cloned.1.call-done = bf16[4096,4096]{1,0:T(8,128)(2,1)} async-done(((bf16[512,4096]{1,0:T(8,128)(2,1)}), bf16[4096,4096]{1,0:T(8,128)(2,1)}) %all-gather.6.cloned.1.call-update) | async-done | bytes 33554448 | tf_op jit(solution)/shard_map/all_gather | solution.py:128
  530.0 14.2 %reduce_sum.41 = bf16[512,4096]{1,0:T(8,128)(2,1)} reduce(bf16[8,512,4096]{2,1,0:T(8,128)(2,1)} %bitcast.100, bf16[]{:T(256)} %constant.60.clone.1), dimensions={0}, to_apply=%region_6.7 | reduce | flops 14680064 | bytes 37748736 | tf_op jit(solution)/shard_map/reduce_sum | solution.py:128
  544.2 1.9 convert_convert_fusion
  (119 shorter events, 40.2 us)
Async XLA Ops:
  6.5 6.4 %copy-start = (bf16[512,512]{1,0:T(8,128)(2,1)S(1)}, bf16[512,512]{1,0:T(8,128)(2,1)}, u32[]{:S(2)}) copy-start(bf16[512,512]{1,0:T(8,128)(2,1)} %param.11) | copy-start | bytes 1572868
  15.0 59.6 %copy-start.1 = (s32[4,512]{1,0:T(4,128)S(1)}, s32[4,512]{1,0:T(4,128)}, u32[]{:S(2)}) copy-start(s32[4,512]{1,0:T(4,128)} %param.13) | copy-start | bytes 24580
  15.9 29.3 %all-to-all-start.2 = ((bf16[4,64,8,128]{3,2,0,1:T(8,128)(2,1)}), bf16[4,64,8,128]{3,2,0,1:T(8,128)(2,1)S(1)}, u32[]{:S(2)}, u32[]{:S(2)}) async-start(bf16[4,64,8,128]{3,2,0,1:T(8,128)(2,1)} %copy.44), calls=%async_computation.2 | async-start | bytes 1048576 | tf_op jit(solution)/shard_map/all_to_all | solution.py:92
  45.2 23.4 %all-to-all-start.1 = ((bf16[4,64,8,128]{3,2,0,1:T(8,128)(2,1)}), bf16[4,64,8,128]{3,2,0,1:T(8,128)(2,1)S(1)}, u32[]{:S(2)}, u32[]{:S(2)}) async-start(bf16[4,64,8,128]{3,2,0,1:T(8,128)(2,1)} %copy.42), calls=%async_computation.1 | async-start | bytes 1048576 | tf_op jit(solution)/shard_map/all_to_all | solution.py:91
  68.7 23.4 %all-to-all-start = ((bf16[4,64,8,128]{3,2,0,1:T(8,128)(2,1)}), bf16[4,64,8,128]{3,2,0,1:T(8,128)(2,1)S(1)}, u32[]{:S(2)}, u32[]{:S(2)}) async-start(bf16[4,64,8,128]{3,2,0,1:T(8,128)(2,1)} %copy.40), calls=%async_computation | async-start | bytes 1048576 | tf_op jit(solution)/shard_map/all_to_all | solution.py:90
  74.4 115.8 %all-gather.4.cloned.1.call-start = ((), (), s32[]{:S(2)}) async-start(), calls=%async_computation.4 | async-start | bytes 4259840 | tf_op jit(solution)/shard_map/all_gather | solution.py:124
  94.8 15.1 %collective-permute-start = (bf16[2,4,512,128]{3,2,1,0:T(8,128)(2,1)S(1)}, bf16[2,4,512,128]{3,2,1,0:T(8,128)(2,1)S(1)}, u32[]{:S(2)}, u32[]{:S(2)}) collective-permute-start(bf16[2,4,512,128]{3,2,1,0:T(8,128)(2,1)S(1)} %pad_maximum_fusion.1), channel_id=1, source_target_pairs={{0,8},{8,16},{16,24},{24,32},{32,40},{40,48},{48,56},{56,64},{64,7... | collective-permute-start | bytes 3145736 | tf_op jit(solution)/shard_map/ppermute | solution.py:18
  98.2 16.2 %collective-permute-start.1 = (bf16[2,4,512,128]{3,2,1,0:T(8,128)(2,1)S(1)}, bf16[2,4,512,128]{3,2,1,0:T(8,128)(2,1)}, u32[]{:S(2)}, u32[]{:S(2)}) collective-permute-start(bf16[2,4,512,128]{3,2,1,0:T(8,128)(2,1)S(1)} %pad_maximum_fusion.1), channel_id=1, source_target_pairs={{8,0},{16,8},{24,16},{32,24},{40,32},{48,40},{56,48},{64,56},{72,6... | collective-permute-start | bytes 3145736 | tf_op jit(solution)/shard_map/ppermute | solution.py:20
  100.1 429.9 %all-gather.6.cloned.1.call-start = ((), (), s32[]{:S(2)}) async-start(), calls=%async_computation.5 | async-start | bytes 37748736 | tf_op jit(solution)/shard_map/all_gather | solution.py:128
Sparse Core Ops, SparseCore 0:
  100.2 89.9 all-gather.3
  197.0 332.9 all-gather.5
